TPU v7x, 32 devices: a whole 2x2x4 slice. The times are simulated.
32 devices in a mesh: groups: 2 (over x), wide: 16 (over z, y, core).
Axes of the slice: x: 2, y: 2, z: 4, core: 2. Of those that a mesh axis runs over, the one named last changes fastest.
Arguments:
- obs_values: bfloat16 [2048, 128, 128], P(('groups', 'wide')), parts along dimension 0, may hold values from -6 to 6
- kernels: bfloat16 [2048, 32, 128], P(('groups', 'wide')), parts along dimension 0, may hold values from -0.5 to 0.5
- block_owner: int32 [2048, 1], P(('groups', 'wide')), parts along dimension 0, may hold values from 0 to 15; in each aligned block of 64 rows (0 to 63, 64 to 127, ...) at most 8 rows name the same one
- block_row: int32 [2048], P(('groups', 'wide')), parts along dimension 0, may hold values from 0 to 7
- valid_count: int32 [2048], P(('groups', 'wide')), parts along dimension 0, may hold values from 1 to 128
- enc_weight: bfloat16 [128, 512], replicated, may hold values from -0.5 to 0.5
- enc_bias: float32 [512], replicated, may hold values from -3 to 3
- conv_weight: bfloat16 [3, 512, 512], replicated, may hold values from -0.15625 to 0.15625
- cotangent: bfloat16 [256, 32, 512], P(('groups', 'wide')), parts along dimension 0, may hold values from -6 to 6
Outputs:
- grid_out: bfloat16 [256, 32, 512], P(('groups', 'wide')), parts along dimension 0
- enc_grad: float32 [256, 512], P('groups'), parts along dimension 0
- conv_grad: float32 [6, 512, 512], P('groups'), parts along dimension 0
There are 2 independent parts, one for each index of `groups`. A program takes and returns all parts, laid end to end along the dimension named above; an argument that names none is the same for every part. Nothing has to cross between parts.
Inputs may be any that keep to these rules, and one draw needn't show every extreme that they name: `block_owner`: among the 64 blocks of one index of wide, at most 8 name the same owner, a bound that some block reaches.
All inputs are finite; a program needn't handle non-finite values.
Results may differ from a plain program's by a relative error of at most 0.0074.
The roundings to bfloat16 on the way count: a program that leaves them out, or rounds other values in their place, can miss the bound.
Values may be sent and summed in bfloat16 or wider, within the bound.
A program may use at most 128 MiB of HBM per device.

v0:
```python
import jax
import jax.numpy as jnp
from jax import lax
from jax.sharding import PartitionSpec as P


def with_halo(block, sides, width):
    for axis, dim in sides:
        count = lax.axis_size(axis)
        forward = [(i, i + 1) for i in range(count - 1)]
        backward = [(target, source) for source, target in forward]
        low = lax.ppermute(
            lax.slice_in_dim(block, block.shape[dim] - width, None, axis=dim), axis, forward
        )
        high = lax.ppermute(lax.slice_in_dim(block, 0, width, axis=dim), axis, backward)
        block = jnp.concatenate([low, block, high], axis=dim)
    return block


def gelu_slope(values):
    return jax.jvp(jax.nn.gelu, (values,), (jnp.ones_like(values),))[1]


def encode_blocks(obs_values, kernels, valid_count, enc_weight, enc_bias):
    pre_act = (
        jnp.einsum("boc,cd->bod", obs_values, enc_weight, preferred_element_type=jnp.float32)
        + enc_bias
    )
    slot_index = lax.broadcasted_iota(jnp.int32, obs_values.shape[:2], 1)
    obs_mask = (slot_index < valid_count[:, None]).astype(jnp.float32)
    hidden = (jax.nn.gelu(pre_act) * obs_mask[:, :, None]).astype(jnp.bfloat16)
    contrib = jnp.einsum(
        "bto,bod->btd", kernels, hidden, preferred_element_type=jnp.float32
    ).astype(jnp.bfloat16)
    return (contrib, pre_act, obs_mask)


def encoder_grad(obs_values, kernels, pre_act, obs_mask, tile_grad):
    hidden_back = jnp.einsum("bto,btd->bod", kernels, tile_grad, preferred_element_type=jnp.float32)
    pre_back = (hidden_back * obs_mask[:, :, None] * gelu_slope(pre_act)).astype(jnp.bfloat16)
    return jnp.einsum("boc,bod->cd", obs_values, pre_back, preferred_element_type=jnp.float32)


def row_mix(rows, weight):
    return jnp.einsum("rtd,de->rte", rows, weight, preferred_element_type=jnp.float32)


def row_outer(left, right):
    return jnp.einsum("rtd,rte->de", left, right, preferred_element_type=jnp.float32)


def local(
    obs_values,
    kernels,
    block_owner,
    block_row,
    valid_count,
    enc_weight,
    enc_bias,
    conv_weight,
    cotangent,
):
    blocks = obs_values.shape[0]
    members = lax.axis_size("wide")
    capacity = max(2, (2 * blocks + members - 1) // members)
    slot_total = members * capacity
    lat_rows, lon_cells, width = cotangent.shape
    owner = block_owner[:, 0]
    owner_hot = (owner[:, None] == lax.broadcasted_iota(jnp.int32, (blocks, members), 1)).astype(
        jnp.int32
    )
    rank_all = jnp.cumsum(owner_hot, axis=0) - owner_hot
    slot_ids = owner * capacity + jnp.sum(rank_all * owner_hot, axis=1)
    row_ids = jnp.full((slot_total,), -1, jnp.int32).at[slot_ids].set(block_row)
    contrib, pre_act, obs_mask = encode_blocks(
        obs_values, kernels, valid_count, enc_weight, enc_bias
    )
    outgoing = jnp.zeros((slot_total, lon_cells, width), jnp.bfloat16).at[slot_ids].set(contrib)
    arrived, arrived_rows = (
        lax.all_to_all(outgoing, "wide", split_axis=0, concat_axis=0, tiled=True),
        lax.all_to_all(row_ids, "wide", split_axis=0, concat_axis=0, tiled=True),
    )
    placing = (
        arrived_rows[None, :] == lax.broadcasted_iota(jnp.int32, (lat_rows, slot_total), 0)
    ).astype(jnp.bfloat16)
    grid = jnp.einsum("rs,std->rtd", placing, arrived, preferred_element_type=jnp.float32).astype(
        jnp.bfloat16
    )
    padded = with_halo(grid, (("wide", 0),), 1)
    conv_in = (
        row_mix(padded[:-2], conv_weight[0])
        + row_mix(padded[1:-1], conv_weight[1])
        + row_mix(padded[2:], conv_weight[2])
    )
    grid_out = (grid.astype(jnp.float32) + jax.nn.gelu(conv_in)).astype(jnp.bfloat16)
    conv_back = (cotangent.astype(jnp.float32) * gelu_slope(conv_in)).astype(jnp.bfloat16)
    weight_terms = jnp.stack(
        [
            row_outer(padded[:-2], conv_back),
            row_outer(padded[1:-1], conv_back),
            row_outer(padded[2:], conv_back),
        ]
    )
    back_pad = with_halo(conv_back, (("wide", 0),), 1)
    grid_back = cotangent.astype(jnp.float32) + row_mix(conv_back, conv_weight[1].T)
    grid_back = (
        grid_back
        + row_mix(back_pad[2:], conv_weight[0].T)
        + row_mix(back_pad[:-2], conv_weight[2].T)
    )
    grid_back = grid_back.astype(jnp.bfloat16)
    safe_rows = jnp.clip(arrived_rows, 0, lat_rows - 1)
    returned = jnp.where(
        (arrived_rows >= 0)[:, None, None], grid_back[safe_rows], jnp.zeros((), jnp.bfloat16)
    )
    coming_back = lax.all_to_all(returned, "wide", split_axis=0, concat_axis=0, tiled=True)
    tile_grad = coming_back[slot_ids]
    enc_part = encoder_grad(obs_values, kernels, pre_act, obs_mask, tile_grad)
    enc_grad, conv_grad = lax.psum((enc_part, weight_terms), "wide")
    return (grid_out, enc_grad, conv_grad)


def solution(mesh):
    in_specs = (
        P(("groups", "wide"), None, None),
        P(("groups", "wide"), None, None),
        P(("groups", "wide"), None),
        P(("groups", "wide")),
        P(("groups", "wide")),
        P(),
        P(),
        P(),
        P(("groups", "wide"), None, None),
    )
    out_specs = (P(("groups", "wide"), None, None), P("groups", None), P("groups", None, None))
    return jax.shard_map(local, mesh=mesh, in_specs=in_specs, out_specs=out_specs, check_vma=False)
```

profile of v0, /device:TPU:0, one launch (start us, length us, event | category | flops | bytes accessed | tf_op | source)
XLA Modules:
  0.0 418.5 jit_solution(12864023161737903488)
XLA Ops:
  7.2 0.9 fusion.51
  8.2 0.8 select_reduce_fusion
  9.0 0.7 fusion.56
  9.7 0.9 scatter_custom_fusion
  10.6 0.7 all_to_all.12
  11.3 7.4 %all-to-all-start = ((s32[16,8,1]{1,2,0:T(1,128)}), s32[16,8,1]{1,2,0:T(1,128)S(1)}, u32[]{:S(2)}, u32[]{:S(2)}) async-start(s32[16,8,1]{1,2,0:T(1,128)} %bitcast.3), calls=%async_computation | async-start | bytes 16384 | tf_op jit(solution)/shard_map/all_to_all | solution.py:81
  18.7 0.7 fusion.52
  19.4 3.3 fusion.49
  22.7 9.5 %convert_bitcast_fusion = bf16[64,32,512]{2,1,0:T(8,128)(2,1)} fusion(bf16[64,32,128]{2,1,0:T(8,128)(2,1)S(1)} %copy-done.4, f32[64,128,512]{2,1,0:T(8,128)S(1)} %fusion.49, f32[64,128]{1,0:T(8,128)S(1)} %fusion.52, f32[512]{0:T(512)S(1)} %copy-done.6), kind=kOutput, calls=%fused_computation.24 | convolution fusion | flops 315621376 | bytes 19433472 | tf_op jit(solution)/shard_map/bto,bod->btd/dot_general | solution.py:32
  32.2 2.5 broadcast_in_dim.11
  34.7 10.0 %scatter_fusion = bf16[128,32,512]{2,1,0:T(8,128)(2,1)} fusion(bf16[128,32,512]{2,1,0:T(8,128)(2,1)} %broadcast_in_dim.11, s32[64]{0:T(128)S(1)} %fusion.56, bf16[64,32,512]{2,1,0:T(8,128)(2,1)} %convert_bitcast_fusion), kind=kCustom, calls=%fused_computation.3 | custom fusion | bytes 6291712 | tf_op jit(solution)/shard_map/scatter | solution.py:78
  44.7 6.0 %all-to-all-start.1 = ((bf16[128,32,512]{2,1,0:T(8,128)(2,1)}), bf16[128,32,512]{2,1,0:T(8,128)(2,1)}, u32[]{:S(2)}, u32[]{:S(2)}) async-start(bf16[128,32,512]{2,1,0:T(8,128)(2,1)} %scatter_fusion), calls=%async_computation.1 | async-start | bytes 8388608 | tf_op jit(solution)/shard_map/all_to_all | solution.py:80
  51.2 0.7 clamp_reduce_fusion
  52.2 76.2 %all-to-all-done.1 = bf16[128,32,512]{2,1,0:T(8,128)(2,1)} async-done(((bf16[128,32,512]{2,1,0:T(8,128)(2,1)}), bf16[128,32,512]{2,1,0:T(8,128)(2,1)}, u32[]{:S(2)}, u32[]{:S(2)}) %all-to-all-start.1) | async-done | bytes 4194336 | tf_op jit(solution)/shard_map/all_to_all | solution.py:80
  128.4 6.8 %fusion.18 = bf16[8,32,512]{2,0,1:T(8,128)(2,1)S(1)} fusion(bf16[128,32,512]{2,1,0:T(8,128)(2,1)} %all-to-all-done.1, s32[128]{0:T(128)S(1)} %eq.23), kind=kOutput, calls=%fused_computation.34 | convolution fusion | flops 33686528 | bytes 4456960 | tf_op jit(solution)/shard_map/rs,std->rtd/dot_general | solution.py:86
  135.2 1.3 collective-permute-start.1
  136.9 3.3 collective-permute-start
  141.1 0.7 fusion.21
  141.9 7.9 %collective-permute-start.3 = (bf16[1,32,512]{2,0,1:T(2,128)(2,1)S(1)}, bf16[1,32,512]{2,0,1:T(2,128)(2,1)S(1)}, u32[]{:S(2)}, u32[]{:S(2)}) collective-permute-start(bf16[1,32,512]{2,0,1:T(2,128)(2,1)S(1)} %get-tuple-element.19), channel_id=1, source_target_pairs={{0,1},{1,2},{2,3},{3,4},{4,5},{5,6},{6,7},{7,8},{8,9},{9,10},{10,1... | collective-permute-start | bytes 98312 | tf_op jit(solution)/shard_map/ppermute | solution.py:12
  150.1 1.3 collective-permute-start.2
  151.8 3.4 collective-permute-done.2
  155.6 2.8 gather_fusion
  158.4 4.5 %broadcast_select_fusion = bf16[128,32,512]{2,1,0:T(8,128)(2,1)} fusion(bf16[128,32,512]{2,1,0:T(8,128)(2,1)} %gather_fusion, pred[128]{0:T(512)(128)(4,1)S(1)} %broadcast_compare_fusion), kind=kLoop, calls=%fused_computation.22 | loop fusion | flops 2097152 | bytes 8388736 | tf_op jit(solution)/shard_map/jit(_where)/select_n | solution.py:113
  162.9 19.8 %all-to-all-start.2 = ((bf16[128,32,512]{2,1,0:T(8,128)(2,1)}), bf16[128,32,512]{2,1,0:T(8,128)(2,1)}, u32[]{:S(2)}, u32[]{:S(2)}) async-start(bf16[128,32,512]{2,1,0:T(8,128)(2,1)} %broadcast_select_fusion), calls=%async_computation.2 | async-start | bytes 8388608 | tf_op jit(solution)/shard_map/all_to_all | solution.py:116
  184.1 2.0 pad_maximum_fusion
  186.0 74.4 %all-to-all-done.2 = bf16[128,32,512]{2,1,0:T(8,128)(2,1)} async-done(((bf16[128,32,512]{2,1,0:T(8,128)(2,1)}), bf16[128,32,512]{2,1,0:T(8,128)(2,1)}, u32[]{:S(2)}, u32[]{:S(2)}) %all-to-all-start.2) | async-done | bytes 4194336 | tf_op jit(solution)/shard_map/all_to_all | solution.py:116
  260.4 4.2 %gather_fusion.1 = bf16[64,32,512]{2,1,0:T(8,128)(2,1)} fusion(bf16[128,32,512]{2,1,0:T(8,128)(2,1)} %all-to-all-done.2, s32[1024]{0:T(1024)S(1)} %pad_clamp_fusion), kind=kCustom, calls=%fused_computation.1 | custom fusion | bytes 4194560 | tf_op jit(solution)/shard_map/gather | solution.py:117
  264.6 20.7 %convolution_bitcast_fusion.3 = f32[128,512]{0,1:T(8,128)} fusion(bf16[64,128,128]{2,1,0:T(8,128)(2,1)S(1)} %copy-done, f32[64,128,512]{2,1,0:T(8,128)} %copy-done.1, bf16[64,32,512]{2,1,0:T(8,128)(2,1)} %gather_fusion.1, bf16[64,32,128]{2,1,0:T(8,128)(2,1)S(1)} %copy-done.5, f32[64,128]{1,0:T(8,128)S(1)} %fusion.52, f32[512]{0:T(512)S(1)} %copy-done.6), kind=kOutput, calls=%fused_computation.35 | convolution fusion | flops 1426063360 | bytes 21792768 | tf_op jit(solution)/shard_map/boc,bod->cd/dot_general | solution.py:41
  285.4 0.8 copy.60
  286.2 119.9 %all-reduce.3.cloned.1.call-done = (f32[128,512]{0,1:T(8,128)}, f32[3,512,512]{2,1,0:T(8,128)}) async-done(((f32[128,512]{0,1:T(8,128)}, f32[3,512,512]{2,1,0:T(8,128)}), (f32[128,512]{0,1:T(8,128)}, f32[3,512,512]{2,1,0:T(8,128)})) %all-reduce.3.cloned.1.call-update) | async-done | bytes 3407888 | tf_op jit(solution)/shard_map/psum | solution.py:119
  406.0 1.8 copy.61
  407.8 3.9 copy.79
  (39 shorter events, 4.6 us)
Async XLA Ops:
  7.2 12.2 %copy-start = (bf16[64,128,128]{2,1,0:T(8,128)(2,1)S(1)}, bf16[64,128,128]{2,1,0:T(8,128)(2,1)}, u32[]{:S(2)}) copy-start(bf16[64,128,128]{2,1,0:T(8,128)(2,1)} %param.9) | copy-start | bytes 6291460
  11.3 33.4 %all-to-all-start = ((s32[16,8,1]{1,2,0:T(1,128)}), s32[16,8,1]{1,2,0:T(1,128)S(1)}, u32[]{:S(2)}, u32[]{:S(2)}) async-start(s32[16,8,1]{1,2,0:T(1,128)} %bitcast.3), calls=%async_computation | async-start | bytes 16384 | tf_op jit(solution)/shard_map/all_to_all | solution.py:81
  19.4 3.3 copy-start.4
  19.4 3.3 copy-start.6
  22.7 9.5 %copy-start.1 = (f32[64,128,512]{2,1,0:T(8,128)}, f32[64,128,512]{2,1,0:T(8,128)S(1)}, u32[]{:S(2)}) copy-start(f32[64,128,512]{2,1,0:T(8,128)S(1)} %fusion.49) | copy-start | bytes 50331652
  44.7 83.7 %all-to-all-start.1 = ((bf16[128,32,512]{2,1,0:T(8,128)(2,1)}), bf16[128,32,512]{2,1,0:T(8,128)(2,1)}, u32[]{:S(2)}, u32[]{:S(2)}) async-start(bf16[128,32,512]{2,1,0:T(8,128)(2,1)} %scatter_fusion), calls=%async_computation.1 | async-start | bytes 8388608 | tf_op jit(solution)/shard_map/all_to_all | solution.py:80
  50.7 90.3 %copy-start.3 = (bf16[8,32,512]{2,1,0:T(8,128)(2,1)S(1)}, bf16[8,32,512]{2,1,0:T(8,128)(2,1)}, u32[]{:S(2)}) copy-start(bf16[8,32,512]{2,1,0:T(8,128)(2,1)} %param.17) | copy-start | bytes 786436
  128.4 8.2 %copy-start.2 = (bf16[3,512,512]{2,1,0:T(8,128)(2,1)S(1)}, bf16[3,512,512]{2,1,0:T(8,128)(2,1)}, u32[]{:S(2)}) copy-start(bf16[3,512,512]{2,1,0:T(8,128)(2,1)} %param.16) | copy-start | bytes 4718596
  135.2 4.9 %collective-permute-start.1 = (bf16[1,32,512]{2,0,1:T(2,128)(2,1)S(1)}, bf16[1,32,512]{2,0,1:T(2,128)(2,1)S(1)}, u32[]{:S(2)}, u32[]{:S(2)}) collective-permute-start(bf16[1,32,512]{2,0,1:T(2,128)(2,1)S(1)} %get-tuple-element.21), channel_id=1, source_target_pairs={{1,0},{2,1},{3,2},{4,3},{5,4},{6,5},{7,6},{8,7},{9,8},{10,9},{11,1... | collective-permute-start | bytes 98312 | tf_op jit(solution)/shard_map/ppermute | solution.py:15
  136.9 4.2 %collective-permute-start = (bf16[1,32,512]{2,0,1:T(2,128)(2,1)S(1)}, bf16[1,32,512]{2,0,1:T(2,128)(2,1)S(1)}, u32[]{:S(2)}, u32[]{:S(2)}) collective-permute-start(bf16[1,32,512]{2,0,1:T(2,128)(2,1)S(1)} %get-tuple-element.20), channel_id=1, source_target_pairs={{0,1},{1,2},{2,3},{3,4},{4,5},{5,6},{6,7},{7,8},{8,9},{9,10},{10,1... | collective-permute-start | bytes 98312 | tf_op jit(solution)/shard_map/ppermute | solution.py:12
  141.9 9.6 %collective-permute-start.3 = (bf16[1,32,512]{2,0,1:T(2,128)(2,1)S(1)}, bf16[1,32,512]{2,0,1:T(2,128)(2,1)S(1)}, u32[]{:S(2)}, u32[]{:S(2)}) collective-permute-start(bf16[1,32,512]{2,0,1:T(2,128)(2,1)S(1)} %get-tuple-element.19), channel_id=1, source_target_pairs={{0,1},{1,2},{2,3},{3,4},{4,5},{5,6},{6,7},{7,8},{8,9},{9,10},{10,1... | collective-permute-start | bytes 98312 | tf_op jit(solution)/shard_map/ppermute | solution.py:12
  150.1 5.0 %collective-permute-start.2 = (bf16[1,32,512]{2,0,1:T(2,128)(2,1)S(1)}, bf16[1,32,512]{2,0,1:T(2,128)(2,1)S(1)}, u32[]{:S(2)}, u32[]{:S(2)}) collective-permute-start(bf16[1,32,512]{2,0,1:T(2,128)(2,1)S(1)} %get-tuple-element.18), channel_id=1, source_target_pairs={{1,0},{2,1},{3,2},{4,3},{5,4},{6,5},{7,6},{8,7},{9,8},{10,9},{11,1... | collective-permute-start | bytes 98312 | tf_op jit(solution)/shard_map/ppermute | solution.py:15
  162.9 97.5 %all-to-all-start.2 = ((bf16[128,32,512]{2,1,0:T(8,128)(2,1)}), bf16[128,32,512]{2,1,0:T(8,128)(2,1)}, u32[]{:S(2)}, u32[]{:S(2)}) async-start(bf16[128,32,512]{2,1,0:T(8,128)(2,1)} %broadcast_select_fusion), calls=%async_computation.2 | async-start | bytes 8388608 | tf_op jit(solution)/shard_map/all_to_all | solution.py:116
  182.7 223.3 %all-reduce.3.cloned.1.call-start = ((), (), s32[]{:S(2)}) async-start(), calls=%async_computation.3 | async-start | bytes 6815744 | tf_op jit(solution)/shard_map/psum | solution.py:119
  184.1 80.6 %copy-start.5 = (bf16[64,32,128]{2,1,0:T(8,128)(2,1)S(1)}, bf16[64,32,128]{2,1,0:T(8,128)(2,1)}, u32[]{:S(2)}) copy-start(bf16[64,32,128]{2,1,0:T(8,128)(2,1)} %param.10) | copy-start | bytes 1572868
Sparse Core Ops, SparseCore 0:
  285.5 120.4 all-reduce.2
where the time goes:
time: 419 us
  waiting for transfers between devices  274 us (65%)
  starting transfers between devices  47.2 us (11%)
  matrix products  43.7 us (10%)
  local copies, waits for them, and re-layouts  28.5 us (7%)
  between operations  14.3 us (3%)
  other arithmetic  10.4 us (2%)
    psum x1, waiting for transfers between devices, local(): enc_grad, conv_grad = lax.psum((enc_part, weight_terms), 'wide')  120 us
    all_to_all x1, waiting for transfers between devices, local(): lax.all_to_all(outgoing, 'wide', split_axis=0, concat_axis=0, tiled=True)  76.2 us
    all_to_all x1, waiting for transfers between devices, local(): lax.all_to_all(returned, 'wide', split_axis=0, concat_axis=0, tiled=True)  74.4 us
    dot_general x1, matrix products, encoder_grad(): jnp.einsum('boc,bod->cd', obs_values, pre_back, preferred_element_type=jn...  20.7 us
    all_to_all x1, starting transfers between devices, local(): lax.all_to_all(returned, 'wide', split_axis=0, concat_axis=0, tiled=True)  19.8 us
    ppermute x2, starting transfers between devices, with_halo(): lax.ppermute(lax.slice_in_dim(block, block.shape[dim] - width, None, axis...  11.2 us
    scatter x1, local copies, waits for them, and re-layouts, local(): jnp.zeros((slot_total, lon_cells, width), jnp.bfloat16).at[slot_ids]  9.97 us
    dot_general x1, matrix products, encode_blocks(): jnp.einsum('bto,bod->btd', kernels, hidden, preferred_element_type=jnp.fl...  9.46 us
  transfers between devices with their start and end apart: 8, of which 5 were waited for; matrix products, arithmetic and copies ran while one was open for 8% of the time, Pallas kernels for 0%

commit v1 on v0

v1 whole, which is shorter than its diff:
```python
import functools
import math

import jax
import jax.numpy as jnp
from jax import lax
from jax.experimental import pallas as pl
from jax.experimental.pallas import tpu as pltpu
from jax.sharding import PartitionSpec as P

F32, BF16 = jnp.float32, jnp.bfloat16
MIB = 1 << 20
ROOT = math.sqrt(2.0 / math.pi)
CUBE = 0.044715


def gelu(x):
    return 0.5 * x * (1.0 + jnp.tanh(ROOT * (x + CUBE * (x * x * x))))


def gelu_slope(x):
    square = x * x
    t = jnp.tanh(ROOT * (x + CUBE * (square * x)))
    return 0.5 * (1.0 + t) + (0.5 * x) * (1.0 - t * t) * (ROOT + (3.0 * CUBE * ROOT) * square)


def dot(left, right, contract=((1,), (0,))):
    return lax.dot_general(left, right, (contract, ((), ())), preferred_element_type=F32)


def orders(bits):
    plain = list(range(bits))
    other = [plain[0], *plain[2:3], *plain[1:2], *plain[3:]]
    return plain, other


def place_of(index, order):
    place = 0
    for bit in order:
        place = place * 2 + index // (1 << bit) % 2
    return place


def mask_of(count, slots):
    return (lax.broadcasted_iota(jnp.int32, (slots, 1), 0) < count).astype(F32)


def encode_kernel(tile_a, tile_b, count, obs, kern, weight, bias, out_a, out_b, acc_a, acc_b):
    blocks, slots, channels = obs.shape
    half = out_a.shape[-1]
    rows = acc_a.shape[0]

    @pl.loop(0, rows)
    def _(r):
        acc_a[r] = jnp.zeros(acc_a.shape[1:], F32)
        acc_b[r] = jnp.zeros(acc_b.shape[1:], F32)

    @pl.loop(0, blocks // 2)
    def _(i):
        for j in range(2):
            b = i * 2 + j
            pre = dot(obs[b], weight[...]) + bias[...]
            hidden = (gelu(pre) * mask_of(count[b], slots)).astype(BF16)
            contrib = dot(kern[b], hidden).astype(BF16).astype(F32)
            acc_a[tile_a[b]] += contrib[:, :half]
            acc_b[tile_b[b]] += contrib[:, half:]

    @pl.loop(0, rows)
    def _(r):
        out_a[r] = acc_a[r].astype(BF16)
        out_b[r] = acc_b[r].astype(BF16)


class Exchange:
    def __init__(self, order, total, me, copies):
        self.me, self.copies = me, copies
        self.partner, self.keep, self.give, self.size = [], [], [], []
        base, size = 0, total
        for bit in order:
            mine = me // (1 << bit) % 2
            size = size // 2
            self.partner.append(me + (1 - 2 * mine) * (1 << bit))
            self.keep.append(base + mine * size)
            self.give.append(base + (1 - mine) * size)
            self.size.append(size)
            base = base + mine * size
        self.pending = {}

    def region(self, ref, offset, size):
        return ref.at[pl.ds(pl.multiple_of(offset, 16), size)]

    def send(self, src, dst, k, tag):
        self.pending[(tag, k)] = self.copies(src, dst, self.partner[k])

    def start_sum(self, k, source, recv, shift=0):
        self.send(self.region(source, self.give[k] - shift, self.size[k]), recv[k], k, "s")

    def finish_sum(self, k, work, recv, shift=0):
        self.pending[("s", k)].wait_recv()
        size, start = self.size[k], self.keep[k] - shift
        step = math.gcd(size, 256)

        @pl.loop(0, size // step)
        def _(i):
            mine = pl.ds(pl.multiple_of(start + i * step, 16), step)
            got = recv[k][pl.ds(pl.multiple_of(i * step, 16), step)]
            work[mine] = (work[mine].astype(F32) + got.astype(F32)).astype(BF16)

    def start_gather(self, k, buffer):
        where = self.region(buffer, self.keep[k], self.size[k])
        self.send(where, where, k, "g")

    def finish_gather(self, k):
        self.pending[("g", k)].wait_recv()

    def drain(self):
        for copy in self.pending.values():
            copy.wait_send()


def grid_kernel(
    members,
    keep_slope,
    tile_a,
    tile_b,
    count,
    dense_a,
    dense_b,
    obs,
    kern,
    weight,
    bias,
    conv_weight,
    cotangent,
    grid_out,
    conv_out,
    enc_out,
    *scratch,
):
    scratch = list(scratch)
    bits = members.bit_length() - 1
    order_a, order_b = orders(bits)
    send_sems, recv_sems, local_sems = scratch.pop(), scratch.pop(), scratch.pop()
    work_a, work_b, gb_a, gb_b, slope, grid_pad, back_pad, cw_a, cw_b, cg_a, cg_b, ew, eg, total = scratch[:14]
    rest = scratch[14:]
    recv_a, recv_b, crecv_a, crecv_b, erecv = [rest[i * bits : (i + 1) * bits] for i in range(5)]

    blocks, slots, channels = obs.shape
    lon = kern.shape[1]
    rows, width = cotangent.shape
    half = width // 2
    me = lax.axis_index("wide")

    used = [0]

    def copies(src, dst, target):
        at = used[0]
        used[0] += 1
        copy = pltpu.make_async_remote_copy(
            src_ref=src,
            dst_ref=dst,
            send_sem=send_sems.at[at],
            recv_sem=recv_sems.at[at],
            device_id={"wide": target},
            device_id_type=pl.DeviceIdType.MESH,
        )
        copy.start()
        return copy

    after, before = lax.rem(me + 1, members), lax.rem(me + members - 1, members)
    grid_rows = members * rows
    sum_a, sum_b = Exchange(order_a, grid_rows, me, copies), Exchange(order_b, grid_rows, me, copies)
    conv_a, conv_b = Exchange(order_a, cw_a.shape[0], me, copies), Exchange(order_b, cw_b.shape[0], me, copies)
    enc = Exchange(order_a, ew.shape[0], me, copies)

    barrier = pltpu.get_barrier_semaphore()
    greeted = [before, after, *sum_a.partner]
    for peer in greeted:
        pl.semaphore_signal(barrier, inc=1, device_id={"wide": peer}, device_id_type=pl.DeviceIdType.MESH)
    pl.semaphore_wait(barrier, len(greeted))

    def slope_of(b):
        pre = dot(obs[b], weight[...]) + bias[...]
        return gelu_slope(pre) * mask_of(count[b], slots)

    def fill_slope(low, high):
        if keep_slope:

            @pl.loop(low, high)
            def _(b):
                slope[b] = slope_of(b)

    streams = ((sum_a, dense_a, work_a, recv_a, gb_a), (sum_b, dense_b, work_b, recv_b, gb_b))
    local = []
    for n, (ex, dense, work, recv, _) in enumerate(streams):
        ex.start_sum(0, dense, recv)
        local.append(
            pltpu.make_async_copy(ex.region(dense, ex.keep[0], ex.size[0]), work, local_sems.at[n])
        )
        local[-1].start()
    cuts = [blocks * k // bits for k in range(bits + 1)]
    fill_slope(cuts[0], cuts[1])
    for k in range(bits):
        for n, (ex, dense, work, recv, _) in enumerate(streams):
            shift = ex.keep[0]
            if k == 0:
                local[n].wait()
            ex.finish_sum(k, work, recv, shift)
            if k + 1 < bits:
                ex.start_sum(k + 1, work, recv, shift)
        if k + 1 < bits:
            fill_slope(cuts[k + 1], cuts[k + 2])

    own = pl.ds(lon, rows)
    for n, (ex, dense, work, recv, _) in enumerate(streams):
        mine = pl.ds(pl.multiple_of(ex.keep[-1] - ex.keep[0], 16), rows)
        grid_pad[own, n * half : (n + 1) * half] = work[mine]

    def halo(pad):
        up = copies(pad.at[pl.ds(rows, lon)], pad.at[pl.ds(0, lon)], after)
        down = copies(pad.at[pl.ds(lon, lon)], pad.at[pl.ds(lon + rows, lon)], before)
        return up, down

    def landed(pad, pair):
        for copy in pair:
            copy.wait_recv()
        first, last = pl.ds(0, lon), pl.ds(lon + rows, lon)
        nothing = jnp.zeros((lon, width), BF16)
        pad[first] = jnp.where(me == 0, nothing, pad[first])
        pad[last] = jnp.where(me == members - 1, nothing, pad[last])

    above, below = pl.ds(0, rows), pl.ds(2 * lon, rows)
    pair = halo(grid_pad)
    conv_in = dot(grid_pad[own], conv_weight[1])
    landed(grid_pad, pair)
    conv_in = conv_in + dot(grid_pad[above], conv_weight[0]) + dot(grid_pad[below], conv_weight[2])
    back_pad[own] = (cotangent[...].astype(F32) * gelu_slope(conv_in)).astype(BF16)
    pair_back = halo(back_pad)
    grid_out[...] = (grid_pad[own].astype(F32) + gelu(conv_in)).astype(BF16)
    turned = ((1,), (1,))
    grid_back = cotangent[...].astype(F32) + dot(back_pad[own], conv_weight[1], turned)
    landed(back_pad, pair_back)
    grid_back = grid_back + dot(back_pad[below], conv_weight[0], turned)
    grid_back = (grid_back + dot(back_pad[above], conv_weight[2], turned)).astype(BF16)
    for n, (ex, _, _, _, gb) in enumerate(streams):
        gb[pl.ds(pl.multiple_of(ex.keep[-1], 16), rows)] = grid_back[:, n * half : (n + 1) * half]
        ex.start_gather(bits - 1, gb)

    outer = ((0,), (0,))
    used_rows = 3 * width
    for k, place in enumerate((above, own, below)):
        term = dot(grid_pad[place], back_pad[own], outer).astype(BF16)
        cw_a[k * width : (k + 1) * width] = term[:, :half]
        cw_b[k * width : (k + 1) * width] = term[:, half:]
    if cw_a.shape[0] > used_rows:
        cw_a[used_rows:] = jnp.zeros((cw_a.shape[0] - used_rows, half), BF16)
        cw_b[used_rows:] = jnp.zeros((cw_b.shape[0] - used_rows, half), BF16)
    conv_streams = ((conv_a, cw_a, crecv_a, cg_a), (conv_b, cw_b, crecv_b, cg_b))
    for ex, cw, recv, _ in conv_streams:
        ex.start_sum(0, cw, recv)
    for k in range(bits):
        for ex, _, _, _, gb in streams:
            ex.finish_gather(bits - 1 - k)
            if k + 1 < bits:
                ex.start_gather(bits - 2 - k, gb)
        for ex, cw, recv, cg in conv_streams:
            ex.finish_sum(k, cw, recv)
            if k + 1 < bits:
                ex.start_sum(k + 1, cw, recv)
            else:
                mine = pl.ds(pl.multiple_of(ex.keep[-1], 16), ex.size[-1])
                cg[mine] = cw[mine]
                ex.start_gather(bits - 1, cg)

    total[...] = jnp.zeros_like(total)

    def encoder_steps(low, high):
        @pl.loop(low, high)
        def _(i):
            parts = []
            for j in range(2):
                b = i * 2 + j
                tile = jnp.concatenate([gb_a3[tile_a[b]], gb_b3[tile_b[b]]], axis=-1)
                hidden_back = dot(kern[b], tile, outer)
                factor = slope[b] if keep_slope else slope_of(b)
                parts.append((hidden_back * factor).astype(BF16))
            pair_obs = obs[pl.ds(i * 2, 2)].reshape(2 * slots, channels)
            total[...] += dot(pair_obs, jnp.concatenate(parts, axis=0), outer)

    gb_a3 = gb_a.reshape(grid_rows // lon, lon, half)
    gb_b3 = gb_b.reshape(grid_rows // lon, lon, half)
    cuts = [blocks // 2 * k // bits for k in range(bits + 1)]
    for k in range(bits):
        encoder_steps(cuts[k], cuts[k + 1])
        for ex, _, _, cg in conv_streams:
            ex.finish_gather(bits - 1 - k)
            if k + 1 < bits:
                ex.start_gather(bits - 2 - k, cg)
    ew[:channels] = total[:, :half].astype(BF16)
    ew[channels : 2 * channels] = total[:, half:].astype(BF16)
    if ew.shape[0] > 2 * channels:
        ew[2 * channels :] = jnp.zeros((ew.shape[0] - 2 * channels, half), BF16)
    enc.start_sum(0, ew, erecv)
    conv_out[:, :half] = cg_a[:used_rows]
    conv_out[:, half:] = cg_b[:used_rows]
    for k in range(bits):
        enc.finish_sum(k, ew, erecv)
        if k + 1 < bits:
            enc.start_sum(k + 1, ew, erecv)
    mine = pl.ds(pl.multiple_of(enc.keep[-1], 16), enc.size[-1])
    eg[mine] = ew[mine]
    for k in range(bits):
        enc.start_gather(bits - 1 - k, eg)
        enc.finish_gather(bits - 1 - k)
    enc_out[:, :half] = eg[:channels]
    enc_out[:, half:] = eg[channels : 2 * channels]
    for ex in (sum_a, sum_b, conv_a, conv_b, enc):
        ex.drain()
    for copy in pair + pair_back:
        copy.wait_send()


def local(
    obs_values, kernels, block_owner, block_row, valid_count, enc_weight, enc_bias, conv_weight, cotangent
):
    members = lax.axis_size("wide")
    bits = members.bit_length() - 1
    order_a, order_b = orders(bits)
    blocks, slots, channels = obs_values.shape
    lat_rows, lon, width = cotangent.shape
    half = width // 2
    owner = block_owner[:, 0]
    tile_a = place_of(owner, order_a) * lat_rows + block_row
    tile_b = place_of(owner, order_b) * lat_rows + block_row
    bias = enc_bias.reshape(1, width)
    lat = members * lat_rows
    smem, vmem = pl.BlockSpec(memory_space=pltpu.SMEM), pl.BlockSpec(memory_space=pltpu.VMEM)
    anywhere = pl.BlockSpec(memory_space=pl.ANY)

    dense_a, dense_b = pl.pallas_call(
        encode_kernel,
        out_shape=[jax.ShapeDtypeStruct((lat, lon, half), BF16)] * 2,
        in_specs=[smem] * 3 + [vmem] * 4,
        out_specs=[vmem] * 2,
        scratch_shapes=[pltpu.VMEM((lat, lon, half), F32)] * 2,
        compiler_params=pltpu.CompilerParams(vmem_limit_bytes=58 * MIB),
        name="encode",
    )(tile_a, tile_b, valid_count, obs_values, kernels, enc_weight, bias)

    rows = lat_rows * lon
    keep_slope = lat <= 256
    unit = 16 * members
    conv_rows = -(-3 * width // unit) * unit
    enc_rows = -(-2 * channels // unit) * unit
    grid_rows = members * rows

    def buffers(total):
        return [pltpu.VMEM((total >> (k + 1), half), BF16) for k in range(bits)]

    scratch = [
        pltpu.VMEM((grid_rows // 2, half), BF16),
        pltpu.VMEM((grid_rows // 2, half), BF16),
        pltpu.VMEM((grid_rows, half), BF16),
        pltpu.VMEM((grid_rows, half), BF16),
        pltpu.VMEM((blocks if keep_slope else 1, slots, width), F32),
        pltpu.VMEM((rows + 2 * lon, width), BF16),
        pltpu.VMEM((rows + 2 * lon, width), BF16),
        pltpu.VMEM((conv_rows, half), BF16),
        pltpu.VMEM((conv_rows, half), BF16),
        pltpu.VMEM((conv_rows, half), BF16),
        pltpu.VMEM((conv_rows, half), BF16),
        pltpu.VMEM((enc_rows, half), BF16),
        pltpu.VMEM((enc_rows, half), BF16),
        pltpu.VMEM((channels, width), F32),
        *buffers(grid_rows),
        *buffers(grid_rows),
        *buffers(conv_rows),
        *buffers(conv_rows),
        *buffers(enc_rows),
        pltpu.SemaphoreType.DMA((2,)),
        pltpu.SemaphoreType.DMA((10 * bits + 4,)),
        pltpu.SemaphoreType.DMA((10 * bits + 4,)),
    ]
    grid_out, conv_sum, enc_sum = pl.pallas_call(
        functools.partial(grid_kernel, members, keep_slope),
        out_shape=[
            jax.ShapeDtypeStruct((rows, width), BF16),
            jax.ShapeDtypeStruct((3 * width, width), BF16),
            jax.ShapeDtypeStruct((channels, width), BF16),
        ],
        in_specs=[smem] * 3 + [anywhere] * 2 + [vmem] * 6,
        out_specs=[vmem] * 3,
        scratch_shapes=scratch,
        compiler_params=pltpu.CompilerParams(
            collective_id=0, has_side_effects=True, vmem_limit_bytes=60 * MIB
        ),
        name="grid",
    )(
        tile_a,
        tile_b,
        valid_count,
        dense_a.reshape(grid_rows, half),
        dense_b.reshape(grid_rows, half),
        obs_values,
        kernels,
        enc_weight,
        bias,
        conv_weight,
        cotangent.reshape(rows, width),
    )
    return (
        grid_out.reshape(cotangent.shape),
        enc_sum.astype(F32),
        conv_sum.astype(F32).reshape(3, width, width),
    )


def solution(mesh):
    in_specs = (
        P(("groups", "wide"), None, None),
        P(("groups", "wide"), None, None),
        P(("groups", "wide"), None),
        P(("groups", "wide")),
        P(("groups", "wide")),
        P(),
        P(),
        P(),
        P(("groups", "wide"), None, None),
    )
    out_specs = (P(("groups", "wide"), None, None), P("groups", None), P("groups", None, None))
    return jax.shard_map(local, mesh=mesh, in_specs=in_specs, out_specs=out_specs, check_vma=False)
```

time: 419 us -> 164 us (0.39)
  waiting for transfers between devices: 274 us -> 0 us
  Pallas kernels: 0 us -> 155 us
  starting transfers between devices: 47.2 us -> 0 us
  matrix products: 43.7 us -> 0 us
  local copies, waits for them, and re-layouts: 28.5 us -> 0.71 us
  between operations: 14.3 us -> 0.64 us
    pallas_call x0 -> x2, Pallas kernels: none -> 155 us  [the longest x1 129 us: local(): pl.pallas_call(functools.partial(grid_kernel, members, keep_slope), out_s...]
    all_to_all x3 -> x0, waiting for transfers between devices: 151 us -> none  [the longest x1 76.2 us: local(): lax.all_to_all(outgoing, 'wide', split_axis=0, concat_axis=0, tiled=True)]
    psum x1 -> x0, waiting for transfers between devices: 120 us -> none  [local(): enc_grad, conv_grad = lax.psum((enc_part, weight_terms), 'wide')]
    dot_general x13 -> x0, matrix products: 43.7 us -> none  [the longest x1 20.7 us: encoder_grad(): jnp.einsum('boc,bod->cd', obs_values, pre_back, preferred_element_type=jn...]
    all_to_all x3 -> x0, starting transfers between devices: 33.2 us -> none  [the longest x1 19.8 us: local(): lax.all_to_all(returned, 'wide', split_axis=0, concat_axis=0, tiled=True)]
    ppermute x4 -> x0, starting transfers between devices: 13.8 us -> none  [the longest x2 11.2 us: with_halo(): lax.ppermute(lax.slice_in_dim(block, block.shape[dim] - width, None, axis...]
    scatter x2 -> x0, local copies, waits for them, and re-layouts: 10.9 us -> none  [the longest x1 9.97 us: local(): jnp.zeros((slot_total, lon_cells, width), jnp.bfloat16).at[slot_ids]]
    gather x2 -> x0, local copies, waits for them, and re-layouts: 6.99 us -> none  [the longest x1 4.19 us: local(): tile_grad = coming_back[slot_ids]]
  transfers between devices with their start and end apart: 8 -> 0, of which waited for: 5 -> 0; matrix products, arithmetic and copies ran while one was open for 8% -> 0% of each run, Pallas kernels for 0% -> 0%
where the time goes in v1:
time: 164 us
  Pallas kernels  155 us (95%)
  other arithmetic  7.59 us (5%)
    pallas_call x1, Pallas kernels, local(): pl.pallas_call(functools.partial(grid_kernel, members, keep_slope), out_s...  129 us
    pallas_call x1, Pallas kernels, local(): pl.pallas_call(encode_kernel, out_shape=[jax.ShapeDtypeStruct((lat, lon,...  25.8 us
    reshape x1, other arithmetic, local(): conv_sum.astype(F32).reshape(3, width, width)  3.56 us

profile of v1, /device:TPU:0, one launch (start us, length us, event | category | flops | bytes accessed | tf_op | source)
XLA Modules:
  0.0 164.1 jit_solution(15572510031378029763)
XLA Ops:
  0.6 1.2 multiply_add_fusion
  1.8 1.2 multiply_add_fusion.1.tile_a
  3.0 25.8 %encode.1 = (bf16[128,32,256]{2,1,0:T(8,128)(2,1)}, bf16[128,32,256]{2,1,0:T(8,128)(2,1)}) custom-call(s32[64]{0:T(128)} %multiply_add_fusion.1.tile_a, s32[64]{0:T(128)} %get-tuple-element.13.tile_b, s32[64]{0:T(128)} %count.3, bf16[64,128,128]{2,1,0:T(8,128)(2,1)} %obs.3, bf16[64,32,128]{2,1,0:T(8,128)(2,1)} %kern.3, bf16[128,512]{1,0:T(8,128)(2,1)} %weight.3, ...), custom_call_target="tpu_custom_call" | custom-call | tf_op jit(solution)/shard_map/encode/pallas_call | solution.py:340
  28.8 129.4 %grid.1 = (bf16[256,512]{1,0:T(8,128)(2,1)}, bf16[1536,512]{1,0:T(8,128)(2,1)}, bf16[128,512]{1,0:T(8,128)(2,1)}) custom-call(s32[64]{0:T(128)} %multiply_add_fusion.1.tile_a, s32[64]{0:T(128)} %get-tuple-element.13.tile_b, s32[64]{0:T(128)} %count.3, bf16[4096,256]{1,0:T(8,128)(2,1)} %bitcast.44, bf16[4096,256]{1,0:T(8,128)(2,1)} %bitcast.45, ...), custom_call_target="tpu_custom_call" | custom-call | tf_op jit(solution)/shard_map/grid/pallas_call | solution.py:384
  158.2 1.6 convert_element_type.4
  159.9 0.0 copy-start
  159.9 3.6 %convert.1 = f32[3,512,512]{2,1,0:T(8,128)} convert(bf16[3,512,512]{2,1,0:T(8,128)(2,1)} %bitcast.46) | non-fusion elementwise | flops 786432 | bytes 4718592 | tf_op jit(solution)/shard_map/reshape | solution.py:414
  163.4 0.0 copy-done
  163.4 0.7 copy.13
Async XLA Ops:
  159.9 3.6 %copy-start = (bf16[256,512]{1,0:T(8,128)(2,1)S(1)}, bf16[256,512]{1,0:T(8,128)(2,1)}, u32[]{:S(2)}) copy-start(bf16[256,512]{1,0:T(8,128)(2,1)} %get-tuple-element.10) | copy-start | bytes 786436

commit v2 on v1

--- a/solution.py
+++ b/solution.py
@@ -15,13 +15,15 @@
 
 
 def gelu(x):
-    return 0.5 * x * (1.0 + jnp.tanh(ROOT * (x + CUBE * (x * x * x))))
+    half = 0.5 * x
+    return half + half * jnp.tanh(x * (ROOT + (ROOT * CUBE) * (x * x)))
 
 
 def gelu_slope(x):
     square = x * x
-    t = jnp.tanh(ROOT * (x + CUBE * (square * x)))
-    return 0.5 * (1.0 + t) + (0.5 * x) * (1.0 - t * t) * (ROOT + (3.0 * CUBE * ROOT) * square)
+    t = jnp.tanh(x * (ROOT + (ROOT * CUBE) * square))
+    bend = x * (0.5 * ROOT + (1.5 * CUBE * ROOT) * square)
+    return 0.5 + 0.5 * t + bend * (1.0 - t * t)
 
 
 def dot(left, right, contract=((1,), (0,))):
@@ -41,8 +43,9 @@
     return place
 
 
-def mask_of(count, slots):
-    return (lax.broadcasted_iota(jnp.int32, (slots, 1), 0) < count).astype(F32)
+def live_part(kern, count):
+    live = lax.broadcasted_iota(jnp.int32, kern.shape, 1) < count
+    return jnp.where(live, kern, jnp.zeros_like(kern))
 
 
 def encode_kernel(tile_a, tile_b, count, obs, kern, weight, bias, out_a, out_b, acc_a, acc_b):
@@ -60,8 +63,8 @@
         for j in range(2):
             b = i * 2 + j
             pre = dot(obs[b], weight[...]) + bias[...]
-            hidden = (gelu(pre) * mask_of(count[b], slots)).astype(BF16)
-            contrib = dot(kern[b], hidden).astype(BF16).astype(F32)
+            hidden = gelu(pre).astype(BF16)
+            contrib = dot(live_part(kern[b], count[b]), hidden).astype(BF16).astype(F32)
             acc_a[tile_a[b]] += contrib[:, :half]
             acc_b[tile_b[b]] += contrib[:, half:]
 
@@ -95,16 +98,31 @@
     def start_sum(self, k, source, recv, shift=0):
         self.send(self.region(source, self.give[k] - shift, self.size[k]), recv[k], k, "s")
 
-    def finish_sum(self, k, work, recv, shift=0):
-        self.pending[("s", k)].wait_recv()
-        size, start = self.size[k], self.keep[k] - shift
+    def start_rounded(self, source, stage, recv):
+        self.add(stage, 0, [(source, self.give[0])], self.size[0])
+        self.send(stage, recv[0], 0, "s")
+
+    @staticmethod
+    def add(out, at, terms, size):
         step = math.gcd(size, 256)
 
         @pl.loop(0, size // step)
         def _(i):
-            mine = pl.ds(pl.multiple_of(start + i * step, 16), step)
-            got = recv[k][pl.ds(pl.multiple_of(i * step, 16), step)]
-            work[mine] = (work[mine].astype(F32) + got.astype(F32)).astype(BF16)
+            parts = [
+                ref[pl.ds(pl.multiple_of(start + i * step, 16), step)].astype(F32)
+                for ref, start in terms
+            ]
+            place = pl.ds(pl.multiple_of(at + i * step, 16), step)
+            out[place] = sum(parts[1:], parts[0]).astype(out.dtype)
+
+    def finish_sum(self, k, source, out, recv, shift=0):
+        self.pending[("s", k)].wait_recv()
+        base, keep, size = self.keep[k], self.keep[k], self.size[k]
+        if ("s", k) != ("s", len(self.size) - 1):
+            give, keep, size = self.give[k + 1], self.keep[k + 1], self.size[k + 1]
+            self.add(recv[k], give - base, [(source, give - shift), (recv[k], give - base)], size)
+            self.send(self.region(recv[k], give - base, size), recv[k + 1], k + 1, "s")
+        self.add(out, keep - shift, [(source, keep - shift), (recv[k], keep - base)], size)
 
     def start_gather(self, k, buffer):
         where = self.region(buffer, self.keep[k], self.size[k])
@@ -115,6 +133,52 @@
 
     def drain(self):
         for copy in self.pending.values():
+            copy.wait_send()
+
+
+class ShortExchange:
+    def __init__(self, bits, total, me, copies):
+        self.copies, self.sent, self.levels = copies, [], []
+        base, size = 0, total
+        for low in range(0, bits, 2):
+            unit, ways = 1 << low, 1 << min(2, bits - low)
+            digit = me // unit % ways
+            size = size // ways
+            others = [lax.rem(digit + d, ways) for d in range(1, ways)]
+            peers = [(other, me + (other - digit) * unit) for other in others]
+            self.levels.append((base, digit, size, peers))
+            base = base + digit * size
+        self.base, self.size = base, size
+
+    def peers(self):
+        return [peer for level in self.levels for _, peer in level[3]]
+
+    def sum(self, k, work, stage, recv):
+        base, digit, size, peers = self.levels[k]
+        Exchange.add(stage[k], 0, [(work, base)], size * (len(peers) + 1))
+        pending = [
+            self.copies(stage[k].at[pl.ds(pl.multiple_of(other * size, 16), size)], recv[k].at[d], peer)
+            for d, (other, peer) in enumerate(peers)
+        ]
+        self.sent += pending
+        mine = pl.ds(pl.multiple_of(base + digit * size, 16), size)
+        for copy in pending:
+            copy.wait_recv()
+        total = work[mine]
+        for d in range(len(peers)):
+            total = total + recv[k][d].astype(F32)
+        work[mine] = total
+
+    def gather(self, k, buffer):
+        base, digit, size, peers = self.levels[k]
+        mine = buffer.at[pl.ds(pl.multiple_of(base + digit * size, 16), size)]
+        pending = [self.copies(mine, mine, peer) for _, peer in peers]
+        self.sent += pending
+        for copy in pending:
+            copy.wait_recv()
+
+    def drain(self):
+        for copy in self.sent:
             copy.wait_send()
 
 
@@ -141,9 +205,12 @@
     bits = members.bit_length() - 1
     order_a, order_b = orders(bits)
     send_sems, recv_sems, local_sems = scratch.pop(), scratch.pop(), scratch.pop()
-    work_a, work_b, gb_a, gb_b, slope, grid_pad, back_pad, cw_a, cw_b, cg_a, cg_b, ew, eg, total = scratch[:14]
-    rest = scratch[14:]
-    recv_a, recv_b, crecv_a, crecv_b, erecv = [rest[i * bits : (i + 1) * bits] for i in range(5)]
+    work_a, work_b, gb_a, gb_b, slope, grid_pad, back_pad, cw_a, cw_b, cs_a, cs_b, cg_a, cg_b, ew, eg, total = scratch[:16]
+    acc_a, acc_b = scratch[16:18] if keep_slope else (work_a, work_b)
+    rest = scratch[18:] if keep_slope else scratch[16:]
+    recv_a, recv_b, crecv_a, crecv_b = [rest[i * bits : (i + 1) * bits] for i in range(4)]
+    levels = (bits + 1) // 2
+    estage, erecv = rest[4 * bits : 4 * bits + levels], rest[4 * bits + levels :]
 
     blocks, slots, channels = obs.shape
     lon = kern.shape[1]
@@ -171,17 +238,17 @@
     grid_rows = members * rows
     sum_a, sum_b = Exchange(order_a, grid_rows, me, copies), Exchange(order_b, grid_rows, me, copies)
     conv_a, conv_b = Exchange(order_a, cw_a.shape[0], me, copies), Exchange(order_b, cw_b.shape[0], me, copies)
-    enc = Exchange(order_a, ew.shape[0], me, copies)
+    enc = ShortExchange(bits, ew.shape[0], me, copies)
 
     barrier = pltpu.get_barrier_semaphore()
-    greeted = [before, after, *sum_a.partner]
+    greeted = [before, after, *enc.peers()]
     for peer in greeted:
         pl.semaphore_signal(barrier, inc=1, device_id={"wide": peer}, device_id_type=pl.DeviceIdType.MESH)
     pl.semaphore_wait(barrier, len(greeted))
 
     def slope_of(b):
         pre = dot(obs[b], weight[...]) + bias[...]
-        return gelu_slope(pre) * mask_of(count[b], slots)
+        return gelu_slope(pre)
 
     def fill_slope(low, high):
         if keep_slope:
@@ -191,6 +258,7 @@
                 slope[b] = slope_of(b)
 
     streams = ((sum_a, dense_a, work_a, recv_a, gb_a), (sum_b, dense_b, work_b, recv_b, gb_b))
+    sums = (acc_a, acc_b)
     local = []
     for n, (ex, dense, work, recv, _) in enumerate(streams):
         ex.start_sum(0, dense, recv)
@@ -205,16 +273,14 @@
             shift = ex.keep[0]
             if k == 0:
                 local[n].wait()
-            ex.finish_sum(k, work, recv, shift)
-            if k + 1 < bits:
-                ex.start_sum(k + 1, work, recv, shift)
+            ex.finish_sum(k, work if k == 0 else sums[n], sums[n], recv, shift)
         if k + 1 < bits:
             fill_slope(cuts[k + 1], cuts[k + 2])
 
     own = pl.ds(lon, rows)
     for n, (ex, dense, work, recv, _) in enumerate(streams):
         mine = pl.ds(pl.multiple_of(ex.keep[-1] - ex.keep[0], 16), rows)
-        grid_pad[own, n * half : (n + 1) * half] = work[mine]
+        grid_pad[own, n * half : (n + 1) * half] = sums[n][mine].astype(BF16)
 
     def halo(pad):
         up = copies(pad.at[pl.ds(rows, lon)], pad.at[pl.ds(0, lon)], after)
@@ -249,28 +315,34 @@
     outer = ((0,), (0,))
     used_rows = 3 * width
     for k, place in enumerate((above, own, below)):
-        term = dot(grid_pad[place], back_pad[own], outer).astype(BF16)
+        term = dot(grid_pad[place], back_pad[own], outer).astype(cw_a.dtype)
         cw_a[k * width : (k + 1) * width] = term[:, :half]
         cw_b[k * width : (k + 1) * width] = term[:, half:]
     if cw_a.shape[0] > used_rows:
-        cw_a[used_rows:] = jnp.zeros((cw_a.shape[0] - used_rows, half), BF16)
-        cw_b[used_rows:] = jnp.zeros((cw_b.shape[0] - used_rows, half), BF16)
+        cw_a[used_rows:] = jnp.zeros((cw_a.shape[0] - used_rows, half), cw_a.dtype)
+        cw_b[used_rows:] = jnp.zeros((cw_b.shape[0] - used_rows, half), cw_b.dtype)
     conv_streams = ((conv_a, cw_a, crecv_a, cg_a), (conv_b, cw_b, crecv_b, cg_b))
-    for ex, cw, recv, _ in conv_streams:
-        ex.start_sum(0, cw, recv)
+    for (ex, cw, recv, _), stage in zip(conv_streams, (cs_a, cs_b)):
+        ex.start_rounded(cw, stage, recv)
     for k in range(bits):
         for ex, _, _, _, gb in streams:
             ex.finish_gather(bits - 1 - k)
             if k + 1 < bits:
                 ex.start_gather(bits - 2 - k, gb)
+        if k > 0:
+            for ex, cw, recv, _ in conv_streams:
+                ex.finish_sum(k - 1, cw, cw, recv)
+
+    def conv_step(k):
         for ex, cw, recv, cg in conv_streams:
-            ex.finish_sum(k, cw, recv)
-            if k + 1 < bits:
-                ex.start_sum(k + 1, cw, recv)
+            if k == 0:
+                ex.finish_sum(bits - 1, cw, cw, recv)
+                mine = pl.ds(pl.multiple_of(ex.keep[-1], 16), ex.size[-1])
+                cg[mine] = cw[mine].astype(BF16)
             else:
-                mine = pl.ds(pl.multiple_of(ex.keep[-1], 16), ex.size[-1])
-                cg[mine] = cw[mine]
-                ex.start_gather(bits - 1, cg)
+                ex.finish_gather(bits - k)
+            if k < bits:
+                ex.start_gather(bits - 1 - k, cg)
 
     total[...] = jnp.zeros_like(total)
 
@@ -281,7 +353,7 @@
             for j in range(2):
                 b = i * 2 + j
                 tile = jnp.concatenate([gb_a3[tile_a[b]], gb_b3[tile_b[b]]], axis=-1)
-                hidden_back = dot(kern[b], tile, outer)
+                hidden_back = dot(live_part(kern[b], count[b]), tile, outer)
                 factor = slope[b] if keep_slope else slope_of(b)
                 parts.append((hidden_back * factor).astype(BF16))
             pair_obs = obs[pl.ds(i * 2, 2)].reshape(2 * slots, channels)
@@ -290,28 +362,33 @@
     gb_a3 = gb_a.reshape(grid_rows // lon, lon, half)
     gb_b3 = gb_b.reshape(grid_rows // lon, lon, half)
     cuts = [blocks // 2 * k // bits for k in range(bits + 1)]
+    done = 0
     for k in range(bits):
         encoder_steps(cuts[k], cuts[k + 1])
-        for ex, _, _, cg in conv_streams:
-            ex.finish_gather(bits - 1 - k)
-            if k + 1 < bits:
-                ex.start_gather(bits - 2 - k, cg)
-    ew[:channels] = total[:, :half].astype(BF16)
-    ew[channels : 2 * channels] = total[:, half:].astype(BF16)
+        if k in (bits // 2, bits - 1):
+            conv_step(done)
+            done += 1
+    ew[:channels] = total[:, :half]
+    ew[channels : 2 * channels] = total[:, half:]
     if ew.shape[0] > 2 * channels:
-        ew[2 * channels :] = jnp.zeros((ew.shape[0] - 2 * channels, half), BF16)
-    enc.start_sum(0, ew, erecv)
+        ew[2 * channels :] = jnp.zeros((ew.shape[0] - 2 * channels, half), F32)
+    for k in range(levels):
+        enc.sum(k, ew, estage, erecv)
+        if done <= bits:
+            conv_step(done)
+            done += 1
+    mine = pl.ds(pl.multiple_of(enc.base, 16), enc.size)
+    eg[mine] = ew[mine].astype(BF16)
+    for k in range(levels):
+        enc.gather(levels - 1 - k, eg)
+        if done <= bits:
+            conv_step(done)
+            done += 1
+    while done <= bits:
+        conv_step(done)
+        done += 1
     conv_out[:, :half] = cg_a[:used_rows]
     conv_out[:, half:] = cg_b[:used_rows]
-    for k in range(bits):
-        enc.finish_sum(k, ew, erecv)
-        if k + 1 < bits:
-            enc.start_sum(k + 1, ew, erecv)
-    mine = pl.ds(pl.multiple_of(enc.keep[-1], 16), enc.size[-1])
-    eg[mine] = ew[mine]
-    for k in range(bits):
-        enc.start_gather(bits - 1 - k, eg)
-        enc.finish_gather(bits - 1 - k)
     enc_out[:, :half] = eg[:channels]
     enc_out[:, half:] = eg[channels : 2 * channels]
     for ex in (sum_a, sum_b, conv_a, conv_b, enc):
@@ -357,29 +434,30 @@
     def buffers(total):
         return [pltpu.VMEM((total >> (k + 1), half), BF16) for k in range(bits)]
 
+    held = F32 if keep_slope else BF16
+    levels = [(low, 1 << min(2, bits - low)) for low in range(0, bits, 2)]
+    copies = 8 * bits + 2 * sum(ways - 1 for _, ways in levels) + 4
     scratch = [
-        pltpu.VMEM((grid_rows // 2, half), BF16),
-        pltpu.VMEM((grid_rows // 2, half), BF16),
-        pltpu.VMEM((grid_rows, half), BF16),
-        pltpu.VMEM((grid_rows, half), BF16),
+        *[pltpu.VMEM((grid_rows // 2, half), BF16)] * 2,
+        *[pltpu.VMEM((grid_rows, half), BF16)] * 2,
         pltpu.VMEM((blocks if keep_slope else 1, slots, width), F32),
-        pltpu.VMEM((rows + 2 * lon, width), BF16),
-        pltpu.VMEM((rows + 2 * lon, width), BF16),
-        pltpu.VMEM((conv_rows, half), BF16),
-        pltpu.VMEM((conv_rows, half), BF16),
-        pltpu.VMEM((conv_rows, half), BF16),
-        pltpu.VMEM((conv_rows, half), BF16),
-        pltpu.VMEM((enc_rows, half), BF16),
+        *[pltpu.VMEM((rows + 2 * lon, width), BF16)] * 2,
+        *[pltpu.VMEM((conv_rows, half), held)] * 2,
+        *[pltpu.VMEM((conv_rows // 2, half), BF16)] * 2,
+        *[pltpu.VMEM((conv_rows, half), BF16)] * 2,
+        pltpu.VMEM((enc_rows, half), F32),
         pltpu.VMEM((enc_rows, half), BF16),
         pltpu.VMEM((channels, width), F32),
+        *([pltpu.VMEM((grid_rows // 2, half), F32)] * 2 if keep_slope else []),
         *buffers(grid_rows),
         *buffers(grid_rows),
         *buffers(conv_rows),
         *buffers(conv_rows),
-        *buffers(enc_rows),
+        *[pltpu.VMEM((enc_rows >> low, half), BF16) for low, _ in levels],
+        *[pltpu.VMEM((ways - 1, (enc_rows >> low) // ways, half), BF16) for low, ways in levels],
         pltpu.SemaphoreType.DMA((2,)),
-        pltpu.SemaphoreType.DMA((10 * bits + 4,)),
-        pltpu.SemaphoreType.DMA((10 * bits + 4,)),
+        pltpu.SemaphoreType.DMA((copies,)),
+        pltpu.SemaphoreType.DMA((copies,)),
     ]
     grid_out, conv_sum, enc_sum = pl.pallas_call(
         functools.partial(grid_kernel, members, keep_slope),

time: 164 us -> 158 us (0.963)
  Pallas kernels: 155 us -> 149 us
    pallas_call x1, Pallas kernels: 129 us -> 125 us  [local(): pl.pallas_call(functools.partial(grid_kernel, members, keep_slope), out_s...]
where the time goes in v2:
time: 158 us
  Pallas kernels  149 us (94%)
  other arithmetic  7.59 us (5%)
    pallas_call x1, Pallas kernels, local(): pl.pallas_call(functools.partial(grid_kernel, members, keep_slope), out_s...  125 us
    pallas_call x1, Pallas kernels, local(): pl.pallas_call(encode_kernel, out_shape=[jax.ShapeDtypeStruct((lat, lon,...  24.7 us
    reshape x1, other arithmetic, local(): conv_sum.astype(F32).reshape(3, width, width)  3.56 us

profile of v2, /device:TPU:0, one launch (start us, length us, event | category | flops | bytes accessed | tf_op | source)
XLA Modules:
  0.0 158.3 jit_solution(7694882540042760446)
XLA Ops:
  0.6 1.2 multiply_add_fusion
  1.8 1.2 multiply_add_fusion.1.tile_a
  3.0 24.7 %encode.1 = (bf16[128,32,256]{2,1,0:T(8,128)(2,1)}, bf16[128,32,256]{2,1,0:T(8,128)(2,1)}) custom-call(s32[64]{0:T(128)} %multiply_add_fusion.1.tile_a, s32[64]{0:T(128)} %get-tuple-element.13.tile_b, s32[64]{0:T(128)} %count.3, bf16[64,128,128]{2,1,0:T(8,128)(2,1)} %obs.3, bf16[64,32,128]{2,1,0:T(8,128)(2,1)} %kern.3, bf16[128,512]{1,0:T(8,128)(2,1)} %weight.3, ...), custom_call_target="tpu_custom_call" | custom-call | tf_op jit(solution)/shard_map/encode/pallas_call | solution.py:417
  27.8 124.6 %grid.1 = (bf16[256,512]{1,0:T(8,128)(2,1)}, bf16[1536,512]{1,0:T(8,128)(2,1)}, bf16[128,512]{1,0:T(8,128)(2,1)}) custom-call(s32[64]{0:T(128)} %multiply_add_fusion.1.tile_a, s32[64]{0:T(128)} %get-tuple-element.13.tile_b, s32[64]{0:T(128)} %count.3, bf16[4096,256]{1,0:T(8,128)(2,1)} %bitcast.44, bf16[4096,256]{1,0:T(8,128)(2,1)} %bitcast.45, ...), custom_call_target="tpu_custom_call" | custom-call | tf_op jit(solution)/shard_map/grid/pallas_call | solution.py:462
  152.4 1.6 %convert_element_type.4 = f32[128,512]{1,0:T(8,128)} convert(bf16[128,512]{1,0:T(8,128)(2,1)} %get-tuple-element.11) | non-fusion elementwise | flops 65536 | bytes 393216 | tf_op jit(solution)/shard_map/convert_element_type | solution.py:491
  154.0 0.0 copy-start
  154.0 3.6 %convert.1 = f32[3,512,512]{2,1,0:T(8,128)} convert(bf16[3,512,512]{2,1,0:T(8,128)(2,1)} %bitcast.46) | non-fusion elementwise | flops 786432 | bytes 4718592 | tf_op jit(solution)/shard_map/reshape | solution.py:492
  157.6 0.0 copy-done
  157.6 0.7 copy.13
Async XLA Ops:
  154.0 3.6 %copy-start = (bf16[256,512]{1,0:T(8,128)(2,1)S(1)}, bf16[256,512]{1,0:T(8,128)(2,1)}, u32[]{:S(2)}) copy-start(bf16[256,512]{1,0:T(8,128)(2,1)} %get-tuple-element.10) | copy-start | bytes 786436

commit v3 on v2

--- a/solution.py
+++ b/solution.py
@@ -53,22 +53,22 @@
     half = out_a.shape[-1]
     rows = acc_a.shape[0]
 
-    @pl.loop(0, rows)
+    @pl.loop(0, rows, unroll=4)
     def _(r):
         acc_a[r] = jnp.zeros(acc_a.shape[1:], F32)
         acc_b[r] = jnp.zeros(acc_b.shape[1:], F32)
 
-    @pl.loop(0, blocks // 2)
+    @pl.loop(0, blocks // 4)
     def _(i):
-        for j in range(2):
-            b = i * 2 + j
+        for j in range(4):
+            b = i * 4 + j
             pre = dot(obs[b], weight[...]) + bias[...]
             hidden = gelu(pre).astype(BF16)
             contrib = dot(live_part(kern[b], count[b]), hidden).astype(BF16).astype(F32)
             acc_a[tile_a[b]] += contrib[:, :half]
             acc_b[tile_b[b]] += contrib[:, half:]
 
-    @pl.loop(0, rows)
+    @pl.loop(0, rows, unroll=4)
     def _(r):
         out_a[r] = acc_a[r].astype(BF16)
         out_b[r] = acc_b[r].astype(BF16)

time: 158 us -> 156 us (0.987)
  Pallas kernels: 149 us -> 147 us
    pallas_call x1, Pallas kernels: 24.7 us -> 22.3 us  [local(): pl.pallas_call(encode_kernel, out_shape=[jax.ShapeDtypeStruct((lat, lon,...]
where the time goes in v3:
time: 156 us
  Pallas kernels  147 us (94%)
  other arithmetic  7.59 us (5%)
    pallas_call x1, Pallas kernels, local(): pl.pallas_call(functools.partial(grid_kernel, members, keep_slope), out_s...  125 us
    pallas_call x1, Pallas kernels, local(): pl.pallas_call(encode_kernel, out_shape=[jax.ShapeDtypeStruct((lat, lon,...  22.3 us
    reshape x1, other arithmetic, local(): conv_sum.astype(F32).reshape(3, width, width)  3.56 us

profile of v3, /device:TPU:0, one launch (start us, length us, event | category | flops | bytes accessed | tf_op | source)
XLA Modules:
  0.0 155.9 jit_solution(7789644379820762407)
XLA Ops:
  0.6 1.2 multiply_add_fusion
  1.8 1.2 multiply_add_fusion.1.tile_a
  3.0 22.3 %encode.1 = (bf16[128,32,256]{2,1,0:T(8,128)(2,1)}, bf16[128,32,256]{2,1,0:T(8,128)(2,1)}) custom-call(s32[64]{0:T(128)} %multiply_add_fusion.1.tile_a, s32[64]{0:T(128)} %get-tuple-element.13.tile_b, s32[64]{0:T(128)} %count.3, bf16[64,128,128]{2,1,0:T(8,128)(2,1)} %obs.3, bf16[64,32,128]{2,1,0:T(8,128)(2,1)} %kern.3, bf16[128,512]{1,0:T(8,128)(2,1)} %weight.3, ...), custom_call_target="tpu_custom_call" | custom-call | tf_op jit(solution)/shard_map/encode/pallas_call | solution.py:417
  25.3 124.7 %grid.1 = (bf16[256,512]{1,0:T(8,128)(2,1)}, bf16[1536,512]{1,0:T(8,128)(2,1)}, bf16[128,512]{1,0:T(8,128)(2,1)}) custom-call(s32[64]{0:T(128)} %multiply_add_fusion.1.tile_a, s32[64]{0:T(128)} %get-tuple-element.13.tile_b, s32[64]{0:T(128)} %count.3, bf16[4096,256]{1,0:T(8,128)(2,1)} %bitcast.44, bf16[4096,256]{1,0:T(8,128)(2,1)} %bitcast.45, ...), custom_call_target="tpu_custom_call" | custom-call | tf_op jit(solution)/shard_map/grid/pallas_call | solution.py:462
  150.0 1.6 %convert_element_type.4 = f32[128,512]{1,0:T(8,128)} convert(bf16[128,512]{1,0:T(8,128)(2,1)} %get-tuple-element.11) | non-fusion elementwise | flops 65536 | bytes 393216 | tf_op jit(solution)/shard_map/convert_element_type | solution.py:491
  151.6 0.0 copy-start
  151.6 3.6 %convert.1 = f32[3,512,512]{2,1,0:T(8,128)} convert(bf16[3,512,512]{2,1,0:T(8,128)(2,1)} %bitcast.46) | non-fusion elementwise | flops 786432 | bytes 4718592 | tf_op jit(solution)/shard_map/reshape | solution.py:492
  155.2 0.0 copy-done
  155.2 0.7 copy.13
Async XLA Ops:
  151.6 3.6 %copy-start = (bf16[256,512]{1,0:T(8,128)(2,1)S(1)}, bf16[256,512]{1,0:T(8,128)(2,1)}, u32[]{:S(2)}) copy-start(bf16[256,512]{1,0:T(8,128)(2,1)} %get-tuple-element.10) | copy-start | bytes 786436
